TPU v7x, 32 devices: a whole 2x2x4 slice. The times are simulated.
32 devices in a mesh: tm: 4 (over y, x), height: 8 (over z, core).
Axes of the slice: x: 2, y: 2, z: 4, core: 2. Of those that a mesh axis runs over, the one named last changes fastest.
Arguments:
- queries: bfloat16 [4, 8, 192, 1536], P('tm', 'height'), may hold values from -4.5 to 4.5
- keys: bfloat16 [4, 8, 192, 1536], P('tm', 'height'), may hold values from -4.5 to 4.5
- values: bfloat16 [4, 8, 192, 1536], P('tm', 'height'), may hold values from -6 to 6
- out_grad: bfloat16 [4, 8, 192, 1536], P('tm', 'height'), may hold values from -6 to 6
- tile_counts: int32 [4, 8], replicated, may hold values from 48 to 192, as said below
- clip_ids: int32 [4], replicated, may hold values from 0 to 1, never falling along the last dimension, each value on 1 to 3 neighbouring positions
Outputs:
- query_grad: bfloat16 [4, 8, 192, 1536], P('tm', 'height')
- key_grad: bfloat16 [4, 8, 192, 1536], P('tm', 'height')
- value_grad: bfloat16 [4, 8, 192, 1536], P('tm', 'height')
Inputs may be any that keep to these rules, and one draw needn't show every extreme that they name: `tile_counts`: at least a quarter of a tile's slots are valid; some tile is full.
All inputs are finite; a program needn't handle non-finite values.
Results may differ from a plain program's by a relative error of at most 0.0085.
Values may be sent and summed in bfloat16 or wider, within the bound.
A program may use at most 192 MiB of HBM per device.

v0:
```python
import jax
import jax.numpy as jnp
from jax import lax
from jax.sharding import PartitionSpec as P

HEADS = 12
HEAD = 128
TILE = 192
HD = 1536


def extended(block, sides, width):
    for axis, dim in sides:
        count = lax.axis_size(axis)
        forward = [(i, i + 1) for i in range(count - 1)]
        backward = [(target, source) for source, target in forward]
        low = lax.ppermute(
            lax.slice_in_dim(block, block.shape[dim] - width, None, axis=dim), axis, forward
        )
        high = lax.ppermute(lax.slice_in_dim(block, 0, width, axis=dim), axis, backward)
        block = jnp.concatenate([low, block, high], axis=dim)
    return block


def window_mask(tile_counts, clip_ids, row, col):
    n_time = tile_counts.shape[0]
    n_high = tile_counts.shape[1]
    offsets = jnp.arange(3, dtype=jnp.int32) - 1
    along_t = row + offsets
    along_h = col + offsets
    inside = ((along_t >= 0) & (along_t < n_time))[:, None] & ((along_h >= 0) & (along_h < n_high))[
        None, :
    ]
    clamp_t = jnp.clip(along_t, 0, n_time - 1)
    clamp_h = jnp.clip(along_h, 0, n_high - 1)
    rows_all = jnp.arange(n_time, dtype=jnp.int32)
    cols_all = jnp.arange(n_high, dtype=jnp.int32)
    hits = (clamp_t[:, None, None, None] == rows_all[None, None, :, None]) & (
        clamp_h[None, :, None, None] == cols_all[None, None, None, :]
    )
    counts = jnp.sum(jnp.where(hits, tile_counts[None, None], 0), axis=(2, 3))
    clip_near = jnp.sum(
        jnp.where(clamp_t[:, None] == rows_all[None, :], clip_ids[None, :], 0), axis=1
    )
    same = clip_near == clip_near[1]
    slots = jnp.arange(TILE, dtype=jnp.int32)
    return inside[:, :, None] & same[:, None, None] & (slots[None, None, :] < counts[:, :, None])


def query_side(query, key_win, value_win, cotangent, key_mask, query_mask):
    scale = 1.0 / HEAD**0.5
    q_heads = query.reshape(TILE, HEADS, HEAD)
    k_heads = key_win.reshape(-1, HEADS, HEAD)
    v_heads = value_win.reshape(-1, HEADS, HEAD)
    g_heads = cotangent.reshape(TILE, HEADS, HEAD)
    scores = (
        jnp.einsum("qhd,khd->hqk", q_heads, k_heads, preferred_element_type=jnp.float32) * scale
    )
    scores = jnp.where(key_mask[None, None, :], scores, jnp.float32(-1e30))
    top = jnp.max(scores, axis=-1, keepdims=True)
    lse = top + jnp.log(jnp.sum(jnp.exp(scores - top), axis=-1, keepdims=True))
    probs = jnp.exp(scores - lse) * query_mask[None, :, None].astype(jnp.float32)
    probs_b = probs.astype(jnp.bfloat16)
    attended = jnp.einsum("hqk,khd->qhd", probs_b, v_heads, preferred_element_type=jnp.float32)
    delta = jnp.einsum("qhd,qhd->hq", g_heads.astype(jnp.float32), attended)
    prob_grad = jnp.einsum("qhd,khd->hqk", g_heads, v_heads, preferred_element_type=jnp.float32)
    score_grad = (probs * (prob_grad - delta[:, :, None])).astype(jnp.bfloat16)
    dquery = (
        jnp.einsum("hqk,khd->qhd", score_grad, k_heads, preferred_element_type=jnp.float32) * scale
    ).reshape(TILE, HD)
    dquery = dquery.astype(jnp.bfloat16)
    return (dquery, lse[:, :, 0], delta)


def local(queries, keys, values, out_grad, tile_counts, clip_ids):
    row = lax.axis_index("tm")
    col = lax.axis_index("height")
    visible = window_mask(tile_counts, clip_ids, row, col)
    own_mask = visible[1, 1]
    query = queries.reshape(TILE, HD)
    cotangent = out_grad.reshape(TILE, HD)
    windowed = extended(jnp.stack([keys, values]), (("tm", 1), ("height", 2)), 1)
    key_win = windowed[0].reshape(9 * TILE, HD)
    value_win = windowed[1].reshape(9 * TILE, HD)
    shape_out = (1, 1, TILE, HD)
    near = extended(jnp.stack([queries, out_grad]), (("tm", 1), ("height", 2)), 1)
    dquery, lse, delta = query_side(
        query, key_win, value_win, cotangent, visible.reshape(-1), own_mask
    )
    stats = extended(jnp.stack([lse, delta])[:, None, None], (("tm", 1), ("height", 2)), 1)
    lse_near = stats[0].transpose(2, 0, 1, 3).reshape(HEADS, 9 * TILE)
    delta_near = stats[1].transpose(2, 0, 1, 3).reshape(HEADS, 9 * TILE)
    scale = 1.0 / HEAD**0.5
    q_near = near[0].reshape(9 * TILE, HEADS, HEAD)
    g_near = near[1].reshape(9 * TILE, HEADS, HEAD)
    k_own = keys.reshape(TILE, HEADS, HEAD)
    v_own = values.reshape(TILE, HEADS, HEAD)
    pair_mask = visible.reshape(-1)[:, None] & own_mask[None, :]
    scores = jnp.einsum("qhd,khd->hqk", q_near, k_own, preferred_element_type=jnp.float32) * scale
    probs = jnp.where(pair_mask[None], jnp.exp(scores - lse_near[:, :, None]), jnp.float32(0.0))
    probs_b = probs.astype(jnp.bfloat16)
    prob_grad = jnp.einsum("qhd,khd->hqk", g_near, v_own, preferred_element_type=jnp.float32)
    score_grad = (probs * (prob_grad - delta_near[:, :, None])).astype(jnp.bfloat16)
    score_tiles = score_grad.reshape(HEADS, 9, TILE, TILE)
    probs_tiles = probs_b.reshape(HEADS, 9, TILE, TILE)
    q_tiles = q_near.reshape(9, TILE, HEADS, HEAD)
    g_tiles = g_near.reshape(9, TILE, HEADS, HEAD)
    key_terms = (
        jnp.einsum("hnqk,nqhd->nkhd", score_tiles, q_tiles, preferred_element_type=jnp.float32)
        * scale
    ).astype(jnp.bfloat16)
    value_terms = jnp.einsum(
        "hnqk,nqhd->nkhd", probs_tiles, g_tiles, preferred_element_type=jnp.float32
    ).astype(jnp.bfloat16)
    dkey = jnp.sum(key_terms.astype(jnp.float32), axis=0)
    dvalue = jnp.sum(value_terms.astype(jnp.float32), axis=0)
    key_grad = dkey.reshape(shape_out).astype(jnp.bfloat16)
    value_grad = dvalue.reshape(shape_out).astype(jnp.bfloat16)
    return (dquery.reshape(shape_out), key_grad, value_grad)


def solution(mesh):
    placed = (
        P("tm", "height", None, None),
        P("tm", "height", None, None),
        P("tm", "height", None, None),
        P("tm", "height", None, None),
        P(),
        P(),
    )
    return jax.shard_map(
        local,
        mesh=mesh,
        in_specs=placed,
        out_specs=(
            P("tm", "height", None, None),
            P("tm", "height", None, None),
            P("tm", "height", None, None),
        ),
        check_vma=False,
    )
```

profile of v0, /device:TPU:21, one launch (start us, length us, event | category | flops | bytes accessed | tf_op | source)
XLA Modules:
  0.0 391.7 jit_solution(12808059645628317012)
XLA Ops:
  7.6 23.4 %collective-permute-done.1 = bf16[2,1,1,192,1536]{4,3,2,1,0:T(8,128)(2,1)S(1)} collective-permute-done((bf16[2,1,1,192,1536]{4,3,2,1,0:T(8,128)(2,1)S(1)}, bf16[2,1,1,192,1536]{4,3,2,1,0:T(8,128)(2,1)S(1)}, u32[]{:S(2)}, u32[]{:S(2)}) %collective-permute-start.1) | collective-permute-done | bytes 1179680 | tf_op jit(solution)/shard_map/ppermute | solution.py:20
  30.9 25.2 %collective-permute-done = bf16[2,1,1,192,1536]{4,3,2,1,0:T(8,128)(2,1)S(1)} collective-permute-done((bf16[2,1,1,192,1536]{4,3,2,1,0:T(8,128)(2,1)S(1)}, bf16[2,1,1,192,1536]{4,3,2,1,0:T(8,128)(2,1)S(1)}, u32[]{:S(2)}, u32[]{:S(2)}) %collective-permute-start) | collective-permute-done | bytes 1179680 | tf_op jit(solution)/shard_map/ppermute | solution.py:17
  83.9 13.4 %collective-permute-done.5 = bf16[2,1,1,192,1536]{4,3,2,1,0:T(8,128)(2,1)S(1)} collective-permute-done((bf16[2,1,1,192,1536]{4,3,2,1,0:T(8,128)(2,1)}, bf16[2,1,1,192,1536]{4,3,2,1,0:T(8,128)(2,1)S(1)}, u32[]{:S(2)}, u32[]{:S(2)}) %collective-permute-start.5) | collective-permute-done | bytes 1179680 | tf_op jit(solution)/shard_map/ppermute | solution.py:20
  97.3 22.8 %collective-permute-done.4 = bf16[2,1,1,192,1536]{4,3,2,1,0:T(8,128)(2,1)} collective-permute-done((bf16[2,1,1,192,1536]{4,3,2,1,0:T(8,128)(2,1)}, bf16[2,1,1,192,1536]{4,3,2,1,0:T(8,128)(2,1)}, u32[]{:S(2)}, u32[]{:S(2)}) %collective-permute-start.4) | collective-permute-done | bytes 1179680 | tf_op jit(solution)/shard_map/ppermute | solution.py:17
  129.4 9.1 %pad_maximum_fusion = bf16[2,3,3,192,1536]{4,3,2,1,0:T(8,128)(2,1)} fusion(bf16[2,3,1,192,1536]{4,3,2,1,0:T(8,128)(2,1)} %collective-permute-done.3, bf16[2,1,1,192,1536]{4,3,2,1,0:T(8,128)(2,1)} %copy-done.5, bf16[1,1,1,192,1536]{4,3,2,1,0:T(8,128)(2,1)S(1)} %bitcast.90, bf16[1,1,1,192,1536]{4,3,2,1,0:T(8,128)(2,1)S(1)} %bitcast.93, ...), kind=kLoop, calls=%fused_computation.14 | loop fusion | flops 26542080 | bytes 21233664 | tf_op jit(solution)/shard_map/concatenate | solution.py:21
  138.5 8.9 %fusion.79 = (bf16[1,3,3,192,1536]{4,3,2,1,0:T(8,128)(2,1)}, bf16[1,3,3,192,1536]{4,3,2,1,0:T(8,128)(2,1)}) fusion(bf16[2,3,3,192,1536]{4,3,2,1,0:T(8,128)(2,1)} %pad_maximum_fusion), kind=kLoop, calls=%fused_computation.78 | loop fusion | bytes 21233664 | tf_op jit(solution)/shard_map/slice | solution.py:84
  147.4 10.5 %reshape_reshape_squeeze.12 = bf16[1728,12,128]{2,1,0:T(8,128)(2,1)} reshape(bf16[1,3,3,192,1536]{4,3,2,1,0:T(8,128)(2,1)} %get-tuple-element.6) | data formatting | bytes 10616832 | tf_op jit(solution)/shard_map/reshape;reshape;squeeze | solution.py:53
  157.9 10.5 %reshape_reshape_squeeze.13 = bf16[1728,12,128]{2,1,0:T(8,128)(2,1)} reshape(bf16[1,3,3,192,1536]{4,3,2,1,0:T(8,128)(2,1)} %get-tuple-element.5) | data formatting | bytes 10616832 | tf_op jit(solution)/shard_map/reshape;reshape;squeeze | solution.py:54
  168.4 14.0 %bitcast_reduce_fusion = (f32[12,192]{1,0:T(8,128)S(1)}, f32[12,1728,192]{1,2,0:T(8,128)}) fusion(pred[1728]{0:T(1024)(128)(4,1)S(1)} %and.107, bf16[192,12,128]{2,1,0:T(8,128)(2,1)S(1)} %copy-done.11, bf16[1728,12,128]{2,1,0:T(8,128)(2,1)} %reshape_reshape_squeeze.12), kind=kOutput, calls=%fused_computation.4 | convolution fusion | flops 1031157504 | bytes 21834432 | tf_op jit(solution)/shard_map/qhd,khd->hqk/dot_general | solution.py:57
  182.5 9.2 %fusion.2 = f32[12,192]{1,0:T(8,128)S(1)} fusion(f32[12,1728,192]{1,2,0:T(8,128)} %get-tuple-element.10, f32[12,192]{1,0:T(8,128)S(1)} %get-tuple-element.9, pred[1728]{0:T(1024)(128)(4,1)S(1)} %and.107), kind=kLoop, calls=%fused_computation.6 | loop fusion | flops 15922944 | bytes 15945408 | tf_op jit(solution)/shard_map/reduce_sum | solution.py:61
  193.0 10.2 %fusion.38 = f32[12,192,128]{2,1,0:T(8,128)} fusion(bf16[1728,12,128]{2,1,0:T(8,128)(2,1)} %reshape_reshape_squeeze.13, f32[12,1728,192]{1,2,0:T(8,128)S(1)} %copy-done, f32[192]{0:T(256)S(1)} %convert_element_type.71, f32[12,192]{1,0:T(8,128)S(1)} %log_add_fusion, pred[1728]{0:T(1024)(128)(4,1)S(1)} %and.107), kind=kOutput, calls=%fused_computation.40 | convolution fusion | flops 1039122432 | bytes 22425024 | tf_op jit(solution)/shard_map/hqk,khd->qhd/dot_general | solution.py:64
  210.9 24.9 %fusion.57 = bf16[192,12,128]{2,0,1:T(8,128)(2,1)} fusion(bf16[1728,12,128]{2,1,0:T(8,128)(2,1)} %reshape_reshape_squeeze.12, f32[12,1728,192]{1,2,0:T(8,128)} %get-tuple-element.10, f32[12,192]{1,0:T(8,128)S(1)} %copy.95, f32[192]{0:T(256)S(1)} %convert_element_type.71, f32[12,192]{1,0:T(8,128)S(1)} %log_add_fusion, pred[1728]{0:T(1024)(128)(4,1)S(1)} %and.107, ...), kind=kOutput, calls=%fused_computation.43 | convolution fusion | flops 2066890752 | bytes 27742656 | tf_op jit(solution)/shard_map/hqk,khd->qhd/dot_general | solution.py:69
  235.8 8.7 %pad_maximum_fusion.1 = bf16[2,3,3,192,1536]{4,3,2,1,0:T(8,128)(2,1)} fusion(bf16[2,3,1,192,1536]{4,3,2,1,0:T(8,128)(2,1)} %collective-permute-done.7, bf16[2,1,1,192,1536]{4,3,2,1,0:T(8,128)(2,1)S(1)} %collective-permute-done.5, bf16[1,1,1,192,1536]{4,3,2,1,0:T(8,128)(2,1)S(1)} %bitcast.99, bf16[1,1,1,192,1536]{4,3,2,1,0:T(8,128)(2,1)S(1)} %bitcast.96, ...), kind=kLoop, calls=%fused_computation.15 | loop fusion | flops 26542080 | bytes 21233664 | tf_op jit(solution)/shard_map/concatenate | solution.py:21
  251.0 9.0 %fusion.78 = (bf16[1,3,3,192,1536]{4,3,2,1,0:T(8,128)(2,1)}, bf16[1,3,3,192,1536]{4,3,2,1,0:T(8,128)(2,1)}) fusion(bf16[2,3,3,192,1536]{4,3,2,1,0:T(8,128)(2,1)} %pad_maximum_fusion.1), kind=kLoop, calls=%fused_computation.77 | loop fusion | bytes 21233664 | tf_op jit(solution)/shard_map/slice | solution.py:95
  260.0 10.7 %reshape_squeeze.6 = bf16[1728,12,128]{2,1,0:T(8,128)(2,1)} reshape(bf16[1,3,3,192,1536]{4,3,2,1,0:T(8,128)(2,1)} %get-tuple-element.4) | data formatting | bytes 10616832 | tf_op jit(solution)/shard_map/reshape;squeeze | solution.py:94
  270.7 10.5 %reshape_reshape_squeeze.14 = bf16[9,192,12,128]{3,2,1,0:T(8,128)(2,1)} reshape(bf16[1,3,3,192,1536]{4,3,2,1,0:T(8,128)(2,1)} %get-tuple-element.4) | data formatting | bytes 10616832 | tf_op jit(solution)/shard_map/reshape;reshape;squeeze | solution.py:106
  281.2 10.5 %reshape_squeeze.7 = bf16[1728,12,128]{2,1,0:T(8,128)(2,1)} reshape(bf16[1,3,3,192,1536]{4,3,2,1,0:T(8,128)(2,1)} %get-tuple-element.3) | data formatting | bytes 10616832 | tf_op jit(solution)/shard_map/reshape;squeeze | solution.py:95
  291.7 10.6 %reshape_reshape_squeeze.15 = bf16[9,192,12,128]{3,2,1,0:T(8,128)(2,1)} reshape(bf16[1,3,3,192,1536]{4,3,2,1,0:T(8,128)(2,1)} %get-tuple-element.3) | data formatting | bytes 10616832 | tf_op jit(solution)/shard_map/reshape;reshape;squeeze | solution.py:107
  304.7 17.0 %fusion.6 = (bf16[12,1728,192]{1,2,0:T(8,128)(2,1)}, f32[12,1728,192]{1,2,0:T(8,128)}) fusion(f32[12,1728]{1,0:T(8,128)S(1)} %sub.60, pred[1728,192]{0,1:T(8,128)(4,1)S(1)} %copy-done.9, bf16[192,12,128]{2,1,0:T(8,128)(2,1)S(1)} %copy-done.8, bf16[1728,12,128]{2,1,0:T(8,128)(2,1)} %reshape_squeeze.6), kind=kOutput, calls=%fused_computation.13 | convolution fusion | flops 1035141120 | bytes 30200832 | tf_op jit(solution)/shard_map/qhd,khd->hqk/dot_general | solution.py:99
  321.8 17.5 %multiply_convert_fusion = bf16[12,1728,192]{1,2,0:T(8,128)(2,1)} fusion(f32[12,1728,192]{1,2,0:T(8,128)} %get-tuple-element.12, f32[12,1728]{1,0:T(8,128)S(1)} %sub.63, f32[12,1728]{1,0:T(8,128)S(1)} %sub.60, pred[1728,192]{0,1:T(8,128)(4,1)S(1)} %copy-done.9, bf16[1728,12,128]{2,1,0:T(8,128)(2,1)} %reshape_squeeze.7, bf16[192,12,128]{2,1,0:T(8,128)(2,1)S(1)} %copy-done.10), kind=kOutput, calls=%fused_computation.9 | convolution fusion | flops 1043103744 | bytes 30283776 | tf_op jit(solution)/shard_map/qhd,khd->hqk/dot_general | solution.py:102
  339.3 12.0 %copy.81 = bf16[12,1728,192]{2,1,0:T(8,128)(2,1)} copy(bf16[12,1728,192]{1,2,0:T(8,128)(2,1)} %multiply_convert_fusion) | data formatting | bytes 15925248 | tf_op jit(solution)/shard_map/convert_element_type | solution.py:103
  351.3 12.5 %fusion.16 = bf16[12,128,192]{1,2,0:T(8,128)(2,1)S(1)} fusion(bf16[12,9,192,192]{3,2,1,0:T(8,128)(2,1)} %bitcast.86, bf16[9,192,12,128]{3,2,1,0:T(8,128)(2,1)} %reshape_reshape_squeeze.14), kind=kOutput, calls=%fused_computation.24 | convolution fusion | flops 1026883584 | bytes 13860864 | tf_op jit(solution)/shard_map/hnqk,nqhd->nkhd/dot_general | solution.py:109
  365.4 12.0 %copy.85 = bf16[12,1728,192]{2,1,0:T(8,128)(2,1)} copy(bf16[12,1728,192]{1,2,0:T(8,128)(2,1)} %get-tuple-element.11) | data formatting | bytes 15925248 | tf_op jit(solution)/shard_map/convert_element_type | solution.py:101
  377.4 12.4 %convert_reduce_fusion = bf16[12,128,192]{1,2,0:T(8,128)(2,1)S(1)} fusion(bf16[12,9,192,192]{3,2,1,0:T(8,128)(2,1)} %bitcast.87, bf16[9,192,12,128]{3,2,1,0:T(8,128)(2,1)} %reshape_reshape_squeeze.15), kind=kOutput, calls=%fused_computation.30 | convolution fusion | flops 1024229376 | bytes 13860864 | tf_op jit(solution)/shard_map/hnqk,nqhd->nkhd/dot_general | solution.py:112
  (106 shorter events, 64.9 us)
Async XLA Ops:
  0.6 79.1 %copy-start.1 = (bf16[1,1,192,1536]{3,2,1,0:T(8,128)(2,1)S(1)}, bf16[1,1,192,1536]{3,2,1,0:T(8,128)(2,1)}, u32[]{:S(2)}) copy-start(bf16[1,1,192,1536]{3,2,1,0:T(8,128)(2,1)} %param.8) | copy-start | bytes 1769476
  0.6 77.8 %copy-start.2 = (bf16[1,1,192,1536]{3,2,1,0:T(8,128)(2,1)S(1)}, bf16[1,1,192,1536]{3,2,1,0:T(8,128)(2,1)}, u32[]{:S(2)}) copy-start(bf16[1,1,192,1536]{3,2,1,0:T(8,128)(2,1)} %param.7) | copy-start | bytes 1769476
  0.7 65.5 %copy-start.4 = (bf16[1,1,192,1536]{3,2,1,0:T(8,128)(2,1)S(1)}, bf16[1,1,192,1536]{3,2,1,0:T(8,128)(2,1)}, u32[]{:S(2)}) copy-start(bf16[1,1,192,1536]{3,2,1,0:T(8,128)(2,1)} %param.9) | copy-start | bytes 1769476
  0.7 65.5 %copy-start.3 = (bf16[1,1,192,1536]{3,2,1,0:T(8,128)(2,1)S(1)}, bf16[1,1,192,1536]{3,2,1,0:T(8,128)(2,1)}, u32[]{:S(2)}) copy-start(bf16[1,1,192,1536]{3,2,1,0:T(8,128)(2,1)} %param.6) | copy-start | bytes 1769476
  0.7 72.0 %copy-start.20 = (s32[4]{0:T(128)S(1)}, s32[4]{0:T(128)}, u32[]{:S(2)}) copy-start(s32[4]{0:T(128)} %param.11) | copy-start | bytes 52
  0.7 80.3 %copy-start.19 = (s32[4,8]{1,0:T(4,128)S(1)}, s32[4,8]{1,0:T(4,128)}, u32[]{:S(2)}) copy-start(s32[4,8]{1,0:T(4,128)} %param.10) | copy-start | bytes 388
  2.2 28.7 %collective-permute-start.1 = (bf16[2,1,1,192,1536]{4,3,2,1,0:T(8,128)(2,1)S(1)}, bf16[2,1,1,192,1536]{4,3,2,1,0:T(8,128)(2,1)S(1)}, u32[]{:S(2)}, u32[]{:S(2)}) collective-permute-start(bf16[2,1,1,192,1536]{4,3,2,1,0:T(8,128)(2,1)S(1)} %pad_maximum_fusion.4), channel_id=1, source_target_pairs={{8,0},{16,8},{24,16},{9,1},{17,9},{25,17},{10,2},{18,10},{26,18},{... | collective-permute-start | bytes 3538952 | tf_op jit(solution)/shard_map/ppermute | solution.py:20
  5.3 50.9 %collective-permute-start = (bf16[2,1,1,192,1536]{4,3,2,1,0:T(8,128)(2,1)S(1)}, bf16[2,1,1,192,1536]{4,3,2,1,0:T(8,128)(2,1)S(1)}, u32[]{:S(2)}, u32[]{:S(2)}) collective-permute-start(bf16[2,1,1,192,1536]{4,3,2,1,0:T(8,128)(2,1)S(1)} %pad_maximum_fusion.4), channel_id=1, source_target_pairs={{0,8},{8,16},{16,24},{1,9},{9,17},{17,25},{2,10},{10,18},{18,26},{... | collective-permute-start | bytes 3538952 | tf_op jit(solution)/shard_map/ppermute | solution.py:17
  30.9 35.2 %copy-start.5 = (bf16[2,1,1,192,1536]{4,3,2,1,0:T(8,128)(2,1)}, bf16[2,1,1,192,1536]{4,3,2,1,0:T(8,128)(2,1)S(1)}, u32[]{:S(2)}) copy-start(bf16[2,1,1,192,1536]{4,3,2,1,0:T(8,128)(2,1)S(1)} %collective-permute-done.1) | copy-start | bytes 3538948
  59.6 69.8 %collective-permute-start.3 = (bf16[2,3,1,192,1536]{4,3,2,1,0:T(8,128)(2,1)}, bf16[2,3,1,192,1536]{4,3,2,1,0:T(8,128)(2,1)}, u32[]{:S(2)}, u32[]{:S(2)}) collective-permute-start(bf16[2,3,1,192,1536]{4,3,2,1,0:T(8,128)(2,1)} %pad_maximum_fusion.2), channel_id=1, source_target_pairs={{1,0},{2,1},{3,2},{4,3},{5,4},{6,5},{7,6},{9,8},{10,9},{11,10},{12... | collective-permute-start | bytes 10616840 | tf_op jit(solution)/shard_map/ppermute | solution.py:20
  63.0 66.4 %collective-permute-start.2 = (bf16[2,3,1,192,1536]{4,3,2,1,0:T(8,128)(2,1)}, bf16[2,3,1,192,1536]{4,3,2,1,0:T(8,128)(2,1)}, u32[]{:S(2)}, u32[]{:S(2)}) collective-permute-start(bf16[2,3,1,192,1536]{4,3,2,1,0:T(8,128)(2,1)} %pad_maximum_fusion.2), channel_id=1, source_target_pairs={{0,1},{1,2},{2,3},{3,4},{4,5},{5,6},{6,7},{8,9},{9,10},{10,11},{11... | collective-permute-start | bytes 10616840 | tf_op jit(solution)/shard_map/ppermute | solution.py:17
  67.3 30.0 %collective-permute-start.5 = (bf16[2,1,1,192,1536]{4,3,2,1,0:T(8,128)(2,1)}, bf16[2,1,1,192,1536]{4,3,2,1,0:T(8,128)(2,1)S(1)}, u32[]{:S(2)}, u32[]{:S(2)}) collective-permute-start(bf16[2,1,1,192,1536]{4,3,2,1,0:T(8,128)(2,1)} %pad_maximum_fusion.5), channel_id=1, source_target_pairs={{8,0},{16,8},{24,16},{9,1},{17,9},{25,17},{10,2},{18,10},{26,18},{... | collective-permute-start | bytes 3538952 | tf_op jit(solution)/shard_map/ppermute | solution.py:20
  69.2 50.9 %collective-permute-start.4 = (bf16[2,1,1,192,1536]{4,3,2,1,0:T(8,128)(2,1)}, bf16[2,1,1,192,1536]{4,3,2,1,0:T(8,128)(2,1)}, u32[]{:S(2)}, u32[]{:S(2)}) collective-permute-start(bf16[2,1,1,192,1536]{4,3,2,1,0:T(8,128)(2,1)} %pad_maximum_fusion.5), channel_id=1, source_target_pairs={{0,8},{8,16},{16,24},{1,9},{9,17},{17,25},{2,10},{10,18},{18,26},{... | collective-permute-start | bytes 3538952 | tf_op jit(solution)/shard_map/ppermute | solution.py:17
  123.1 112.6 %collective-permute-start.7 = (bf16[2,3,1,192,1536]{4,3,2,1,0:T(8,128)(2,1)}, bf16[2,3,1,192,1536]{4,3,2,1,0:T(8,128)(2,1)}, u32[]{:S(2)}, u32[]{:S(2)}) collective-permute-start(bf16[2,3,1,192,1536]{4,3,2,1,0:T(8,128)(2,1)} %pad_maximum_fusion.3), channel_id=1, source_target_pairs={{1,0},{2,1},{3,2},{4,3},{5,4},{6,5},{7,6},{9,8},{10,9},{11,10},{12... | collective-permute-start | bytes 10616840 | tf_op jit(solution)/shard_map/ppermute | solution.py:20
  125.1 110.7 %collective-permute-start.6 = (bf16[2,3,1,192,1536]{4,3,2,1,0:T(8,128)(2,1)}, bf16[2,3,1,192,1536]{4,3,2,1,0:T(8,128)(2,1)}, u32[]{:S(2)}, u32[]{:S(2)}) collective-permute-start(bf16[2,3,1,192,1536]{4,3,2,1,0:T(8,128)(2,1)} %pad_maximum_fusion.3), channel_id=1, source_target_pairs={{0,1},{1,2},{2,3},{3,4},{4,5},{5,6},{6,7},{8,9},{9,10},{10,11},{11... | collective-permute-start | bytes 10616840 | tf_op jit(solution)/shard_map/ppermute | solution.py:17
  205.4 39.0 %copy-start.13 = (f32[2,1,1,12,192]{4,0,3,2,1:T(2,128)}, f32[2,1,1,12,192]{4,0,3,2,1:T(2,128)S(1)}, u32[]{:S(2)}) copy-start(f32[2,1,1,12,192]{4,0,3,2,1:T(2,128)S(1)} %maximum_bitcast_fusion) | copy-start | bytes 55300
  205.4 39.0 %collective-permute-start.9 = (f32[2,1,1,12,192]{4,0,3,2,1:T(2,128)S(1)}, f32[2,1,1,12,192]{4,0,3,2,1:T(2,128)S(1)}, u32[]{:S(2)}, u32[]{:S(2)}) collective-permute-start(f32[2,1,1,12,192]{4,0,3,2,1:T(2,128)S(1)} %maximum_bitcast_fusion), channel_id=1, source_target_pairs={{8,0},{16,8},{24,16},{9,1},{17,9},{25,17},{10,2},{18,10},{26,18},{... | collective-permute-start | bytes 55304 | tf_op jit(solution)/shard_map/ppermute | solution.py:20
  207.4 37.1 %collective-permute-start.8 = (f32[2,1,1,12,192]{4,0,3,2,1:T(2,128)S(1)}, f32[2,1,1,12,192]{4,0,3,2,1:T(2,128)S(1)}, u32[]{:S(2)}, u32[]{:S(2)}) collective-permute-start(f32[2,1,1,12,192]{4,0,3,2,1:T(2,128)S(1)} %maximum_bitcast_fusion), channel_id=1, source_target_pairs={{0,8},{8,16},{16,24},{1,9},{9,17},{17,25},{2,10},{10,18},{18,26},{... | collective-permute-start | bytes 55304 | tf_op jit(solution)/shard_map/ppermute | solution.py:17
  244.5 15.6 %copy-start.15 = (f32[2,1,1,12,192]{4,0,3,2,1:T(2,128)}, f32[2,1,1,12,192]{4,0,3,2,1:T(2,128)S(1)}, u32[]{:S(2)}) copy-start(f32[2,1,1,12,192]{4,0,3,2,1:T(2,128)S(1)} %collective-permute-done.9) | copy-start | bytes 55300
  244.5 15.6 %copy-start.17 = (f32[2,1,1,12,192]{4,0,3,2,1:T(2,128)}, f32[2,1,1,12,192]{4,0,3,2,1:T(2,128)S(1)}, u32[]{:S(2)}) copy-start(f32[2,1,1,12,192]{4,0,3,2,1:T(2,128)S(1)} %collective-permute-done.8) | copy-start | bytes 55300
  244.5 59.4 %collective-permute-start.11 = (f32[2,3,1,12,192]{4,0,3,2,1:T(2,128)S(1)}, f32[2,3,1,12,192]{4,0,3,2,1:T(2,128)S(1)}, u32[]{:S(2)}, u32[]{:S(2)}) collective-permute-start(f32[2,3,1,12,192]{4,0,3,2,1:T(2,128)S(1)} %pad_maximum_fusion.7), channel_id=1, source_target_pairs={{1,0},{2,1},{3,2},{4,3},{5,4},{6,5},{7,6},{9,8},{10,9},{11,10},{12... | collective-permute-start | bytes 165896 | tf_op jit(solution)/shard_map/ppermute | solution.py:20
  246.5 57.5 %collective-permute-start.10 = (f32[2,3,1,12,192]{4,0,3,2,1:T(2,128)S(1)}, f32[2,3,1,12,192]{4,0,3,2,1:T(2,128)S(1)}, u32[]{:S(2)}, u32[]{:S(2)}) collective-permute-start(f32[2,3,1,12,192]{4,0,3,2,1:T(2,128)S(1)} %pad_maximum_fusion.7), channel_id=1, source_target_pairs={{0,1},{1,2},{2,3},{3,4},{4,5},{5,6},{6,7},{8,9},{9,10},{10,11},{11... | collective-permute-start | bytes 165896 | tf_op jit(solution)/shard_map/ppermute | solution.py:17
  291.7 13.1 %copy-start.8 = (bf16[192,12,128]{2,1,0:T(8,128)(2,1)S(1)}, bf16[192,12,128]{2,1,0:T(8,128)(2,1)}, u32[]{:S(2)}) copy-start(bf16[192,12,128]{2,1,0:T(8,128)(2,1)} %reshape.297) | copy-start | bytes 1769476
  304.7 17.0 %copy-start.10 = (bf16[192,12,128]{2,1,0:T(8,128)(2,1)S(1)}, bf16[192,12,128]{2,1,0:T(8,128)(2,1)}, u32[]{:S(2)}) copy-start(bf16[192,12,128]{2,1,0:T(8,128)(2,1)} %reshape.298) | copy-start | bytes 1769476
  (9 other events, 103.1 us)
where the time goes:
time: 398 us; the launch traced here: 392 us
  local copies, waits for them, and re-layouts  118 us (30%)
  matrix products  109 us (27%)
  waiting for transfers between devices  84.8 us (21%)
  other arithmetic  43.6 us (11%)
  starting transfers between devices  35.4 us (9%)
    ppermute x6, waiting for transfers between devices, extended(): lax.ppermute(lax.slice_in_dim(block, block.shape[dim] - width, None, axis...  48 us
    ppermute x6, waiting for transfers between devices, extended(): lax.ppermute(lax.slice_in_dim(block, 0, width, axis=dim), axis, backward)  36.7 us
    dot_general x1, matrix products, query_side(): jnp.einsum('hqk,khd->qhd', score_grad, k_heads, preferred_element_type=jn...  24.9 us
    concatenate x6, other arithmetic, extended(): block = jnp.concatenate([low, block, high], axis=dim)  24.4 us
    ppermute x6, starting transfers between devices, extended(): lax.ppermute(lax.slice_in_dim(block, block.shape[dim] - width, None, axis...  21.2 us
    dot_general x1, matrix products, local(): jnp.einsum('qhd,khd->hqk', g_near, v_own, preferred_element_type=jnp.floa...  17.5 us
    dot_general x1, matrix products, local(): jnp.einsum('qhd,khd->hqk', q_near, k_own, preferred_element_type=jnp.floa...  17 us
    ppermute x6, starting transfers between devices, extended(): lax.ppermute(lax.slice_in_dim(block, 0, width, axis=dim), axis, backward)  14.2 us
  transfers between devices with their start and end apart: 12, of which 4 were waited for; matrix products, arithmetic and copies ran while one was open for 45% of the time, Pallas kernels for 0%

commit v1 on v0

--- a/solution.py
+++ b/solution.py
@@ -1,12 +1,420 @@
+import functools
+import math
+
 import jax
 import jax.numpy as jnp
 from jax import lax
+from jax.experimental import pallas as pl
+from jax.experimental.pallas import tpu as pltpu
 from jax.sharding import PartitionSpec as P
 
 HEADS = 12
 HEAD = 128
 TILE = 192
 HD = 1536
+MESH = pl.DeviceIdType.MESH
+SCALE = 1.0 / HEAD**0.5
+ROWS = 4
+PER = HEADS // ROWS
+WIN = 9
+
+
+def head_kernel(
+    n_high,
+    counts,
+    clips,
+    q_in,
+    k_in,
+    v_in,
+    g_in,
+    dq_out,
+    dk_out,
+    dv_out,
+    kv,
+    qg,
+    score,
+    pgrad,
+    dq_t,
+    acc,
+    t_send,
+    t_recv,
+    o_send,
+    in_send,
+    in_recv,
+    kv_send,
+    kv_recv,
+    tr_send,
+    tr_recv,
+    out_send,
+    out_recv,
+):
+    me = lax.axis_index("tm")
+    col = lax.axis_index("height")
+    has_low = col > 0
+    has_high = col < n_high - 1
+    peers = [lax.rem(me + i, ROWS) for i in (1, 2, 3)]
+
+    barrier = pltpu.get_barrier_semaphore()
+    for peer in peers:
+        pl.semaphore_signal(barrier, inc=1, device_id=(peer, col), device_id_type=MESH)
+
+    @pl.when(has_low)
+    def _():
+        pl.semaphore_signal(barrier, inc=1, device_id=(me, col - 1), device_id_type=MESH)
+
+    @pl.when(has_high)
+    def _():
+        pl.semaphore_signal(barrier, inc=1, device_id=(me, col + 1), device_id_type=MESH)
+
+    pl.semaphore_wait(barrier, 3 + has_low.astype(jnp.int32) + has_high.astype(jnp.int32))
+
+    sources = (k_in, v_in, q_in, g_in)
+
+    def landing(j, a, r):
+        return kv.at[j, 1, a, r] if a < 2 else qg.at[j, a - 2, r]
+
+    def in_copy(j, a, peer):
+        start = pl.multiple_of((peer * PER + j) * HEAD, HEAD)
+        return pltpu.make_async_remote_copy(
+            src_ref=sources[a].at[0, 0, :, pl.ds(start, HEAD)],
+            dst_ref=landing(j, a, me),
+            send_sem=in_send.at[j, a, peer],
+            recv_sem=in_recv.at[j, a, me],
+            device_id=(peer, col),
+            device_id_type=MESH,
+        )
+
+    def in_local(j, a):
+        start = pl.multiple_of((me * PER + j) * HEAD, HEAD)
+        return pltpu.make_async_copy(
+            sources[a].at[0, 0, :, pl.ds(start, HEAD)], landing(j, a, me), in_recv.at[j, a, me]
+        )
+
+    def in_arrival(j, a, peer):
+        return pltpu.make_async_remote_copy(
+            src_ref=landing(j, a, peer),
+            dst_ref=landing(j, a, peer),
+            send_sem=in_send.at[j, a, peer],
+            recv_sem=in_recv.at[j, a, peer],
+            device_id=(peer, col),
+            device_id_type=MESH,
+        )
+
+    def start_in(j, _):
+        for a in range(4):
+            for peer in (peers[1], peers[0], peers[2]):
+                in_copy(j, a, peer).start()
+            in_local(j, a).start()
+        return 0
+
+    lax.fori_loop(0, PER, start_in, 0)
+
+    def wait_in(j, arrays):
+        for a in arrays:
+            in_local(j, a).wait()
+            for peer in peers:
+                in_arrival(j, a, peer).wait_recv()
+
+    sides = ((0, has_low, -1), (1, has_high, 1))
+
+    def kv_copy(j, side, step):
+        return pltpu.make_async_remote_copy(
+            src_ref=kv.at[j, 1],
+            dst_ref=kv.at[j, 2 - 2 * side],
+            send_sem=kv_send.at[j, side],
+            recv_sem=kv_recv.at[j, 1 - side],
+            device_id=(me, col + step),
+            device_id_type=MESH,
+        )
+
+    def kv_arrival(j, side, step):
+        return pltpu.make_async_remote_copy(
+            src_ref=kv.at[j, 1],
+            dst_ref=kv.at[j, 2 * side],
+            send_sem=kv_send.at[j, side],
+            recv_sem=kv_recv.at[j, side],
+            device_id=(me, col + step),
+            device_id_type=MESH,
+        )
+
+    def term_copy(j, side, step):
+        return pltpu.make_async_remote_copy(
+            src_ref=t_send.at[j, side],
+            dst_ref=t_recv.at[j, 1 - side],
+            send_sem=tr_send.at[j, side],
+            recv_sem=tr_recv.at[j, 1 - side],
+            device_id=(me, col + step),
+            device_id_type=MESH,
+        )
+
+    def term_arrival(j, side, step):
+        return pltpu.make_async_remote_copy(
+            src_ref=t_send.at[j, side],
+            dst_ref=t_recv.at[j, side],
+            send_sem=tr_send.at[j, side],
+            recv_sem=tr_recv.at[j, side],
+            device_id=(me, col + step),
+            device_id_type=MESH,
+        )
+
+    def forward(j):
+        wait_in(j, (0, 1))
+        for side, there, step in sides:
+
+            @pl.when(there)
+            def _():
+                kv_copy(j, side, step).start()
+
+            @pl.when(jnp.logical_not(there))
+            def _():
+                kv[j, 2 * side] = jnp.zeros((2, ROWS, TILE, HEAD), jnp.bfloat16)
+
+    results = (dq_out, dk_out, dv_out)
+
+    def out_place(j, o, row):
+        start = pl.multiple_of((row * PER + j) * HEAD, HEAD)
+        return results[o].at[0, 0, :, pl.ds(start, HEAD)]
+
+    def out_copy(j, o, peer):
+        return pltpu.make_async_remote_copy(
+            src_ref=o_send.at[j, o, peer],
+            dst_ref=out_place(j, o, me),
+            send_sem=out_send.at[j, o, peer],
+            recv_sem=out_recv.at[j, o, me],
+            device_id=(peer, col),
+            device_id_type=MESH,
+        )
+
+    def out_local(j, o):
+        return pltpu.make_async_copy(
+            o_send.at[j, o, me], out_place(j, o, me), out_send.at[j, o, me]
+        )
+
+    def out_arrival(j, o, peer):
+        return pltpu.make_async_remote_copy(
+            src_ref=o_send.at[j, o, peer],
+            dst_ref=out_place(j, o, peer),
+            send_sem=out_send.at[j, o, peer],
+            recv_sem=out_recv.at[j, o, peer],
+            device_id=(peer, col),
+            device_id_type=MESH,
+        )
+
+    def start_out(j, o):
+        for peer in (peers[1], peers[0], peers[2]):
+            out_copy(j, o, peer).start()
+        out_local(j, o).start()
+
+    lane = lax.broadcasted_iota(jnp.int32, (1, 2 * TILE), 1)
+    first_half = lane < TILE
+    slot = lax.broadcasted_iota(jnp.int32, (TILE, 2 * TILE), 0)
+
+    def visible_count(row, key_row, offset):
+        there = col + offset - 1
+        inside = (there >= 0) & (there < n_high)
+        near = jnp.abs(row - key_row) <= 1
+        same = clips[row] == clips[key_row]
+        count = counts[key_row, jnp.clip(there, 0, n_high - 1)]
+        return jnp.where(inside & near & same, count, 0)
+
+    def fold(x, op):
+        return op(x.reshape(TILE // 8, 8, 2 * TILE), axis=0)
+
+    def block(j, b):
+        row = 2 * b
+        q = qg[j, 0, pl.ds(row, 2)].reshape(2 * TILE, HEAD)
+        g = qg[j, 1, pl.ds(row, 2)].reshape(2 * TILE, HEAD)
+        q_t = q.T
+        g_t = g.T
+
+        def scores(t, top):
+            key_row, offset = b + t // 3, t % 3
+            s = jnp.dot(kv[j, offset, 0, key_row], q_t, preferred_element_type=jnp.float32)
+            limit = jnp.where(
+                first_half,
+                visible_count(row, key_row, offset),
+                visible_count(row + 1, key_row, offset),
+            )
+            s = jnp.where(slot < limit, s * (SCALE * math.log2(math.e)), jnp.float32(-1e30))
+            score[t] = s
+            pgrad[t] = jnp.dot(kv[j, offset, 1, key_row], g_t, preferred_element_type=jnp.float32)
+            return jnp.maximum(top, fold(s, jnp.max))
+
+        top = lax.fori_loop(0, WIN, scores, jnp.full((8, 2 * TILE), -1e30, jnp.float32))
+        top = jnp.max(top, axis=0, keepdims=True)
+
+        def sums(t, carry):
+            total, dot = carry
+            e = jnp.exp2(score[t] - top)
+            score[t] = e
+            return total + fold(e, jnp.sum), dot + fold(e * pgrad[t], jnp.sum)
+
+        zero = jnp.zeros((8, 2 * TILE), jnp.float32)
+        total, dot = lax.fori_loop(0, WIN, sums, (zero, zero))
+        total = jnp.sum(total, axis=0, keepdims=True)
+        dot = jnp.sum(dot, axis=0, keepdims=True)
+        own = jnp.where(first_half, counts[row, col], counts[row + 1, col] + TILE)
+        inverse = 1.0 / total
+        delta = dot * inverse
+        inverse = jnp.where(lane < own, inverse, 0.0)
+        dq_t[...] = jnp.zeros_like(dq_t)
+
+        def grads(t, _):
+            key_row, offset = b + t // 3, t % 3
+            p = score[t] * inverse
+            ds = (p * (pgrad[t] - delta)).astype(jnp.bfloat16)
+            p = p.astype(jnp.bfloat16)
+            k_t = kv[j, offset, 0, key_row].T
+            dq_t[...] += jnp.dot(k_t, ds, preferred_element_type=jnp.float32)
+            fresh = (b == 0) | (key_row == ROWS - 1)
+            old_k = jnp.where(fresh, 0.0, acc[j, offset, 0, key_row])
+            acc[j, offset, 0, key_row] = old_k + jnp.dot(ds, q, preferred_element_type=jnp.float32)
+            old_v = jnp.where(fresh, 0.0, acc[j, offset, 1, key_row])
+            acc[j, offset, 1, key_row] = old_v + jnp.dot(p, g, preferred_element_type=jnp.float32)
+            return 0
+
+        lax.fori_loop(0, WIN, grads, 0)
+        dq = (dq_t[...] * SCALE).T.astype(jnp.bfloat16)
+        o_send[j, 0, pl.ds(row, 2)] = dq.reshape(2, TILE, HEAD)
+
+    def send_terms(j):
+        for side, there, step in sides:
+
+            @pl.when(there)
+            def _():
+                def cast(r, _):
+                    t_send[j, side, 0, r] = (acc[j, 2 * side, 0, r] * SCALE).astype(jnp.bfloat16)
+                    t_send[j, side, 1, r] = acc[j, 2 * side, 1, r].astype(jnp.bfloat16)
+                    return 0
+
+                lax.fori_loop(0, ROWS, cast, 0)
+                term_copy(j, side, step).start()
+
+    def finish(j):
+        for side, there, step in sides:
+
+            @pl.when(there)
+            def _():
+                term_arrival(j, side, step).wait_recv()
+
+            @pl.when(jnp.logical_not(there))
+            def _():
+                t_recv[j, side] = jnp.zeros((2, ROWS, TILE, HEAD), jnp.bfloat16)
+
+        def add(r, _):
+            dk = (
+                acc[j, 1, 0, r] * SCALE
+                + t_recv[j, 0, 0, r].astype(jnp.float32)
+                + t_recv[j, 1, 0, r].astype(jnp.float32)
+            )
+            dv = (
+                acc[j, 1, 1, r]
+                + t_recv[j, 0, 1, r].astype(jnp.float32)
+                + t_recv[j, 1, 1, r].astype(jnp.float32)
+            )
+            o_send[j, 1, r] = dk.astype(jnp.bfloat16)
+            o_send[j, 2, r] = dv.astype(jnp.bfloat16)
+            return 0
+
+        lax.fori_loop(0, ROWS, add, 0)
+        start_out(j, 1)
+        start_out(j, 2)
+
+    forward(0)
+
+    def head(j, _):
+        @pl.when(j + 1 < PER)
+        def _():
+            forward(j + 1)
+
+        wait_in(j, (2, 3))
+        for side, there, step in sides:
+
+            @pl.when(there)
+            def _():
+                kv_arrival(j, side, step).wait_recv()
+
+        def one_block(b, _):
+            block(j, b)
+            return 0
+
+        lax.fori_loop(0, ROWS // 2, one_block, 0)
+        send_terms(j)
+        start_out(j, 0)
+
+        @pl.when(j > 0)
+        def _():
+            finish(j - 1)
+
+        return 0
+
+    lax.fori_loop(0, PER, head, 0)
+    finish(PER - 1)
+
+    def drain(j, _):
+        for a in range(4):
+            for peer in peers:
+                in_copy(j, a, peer).wait_send()
+        for side, there, step in sides:
+
+            @pl.when(there)
+            def _():
+                kv_copy(j, side, step).wait_send()
+                term_copy(j, side, step).wait_send()
+
+        for o in range(3):
+            out_local(j, o).wait()
+            for peer in peers:
+                out_copy(j, o, peer).wait_send()
+                out_arrival(j, o, peer).wait_recv()
+        return 0
+
+    lax.fori_loop(0, PER, drain, 0)
+
+
+def by_heads(n_high, queries, keys, values, out_grad, tile_counts, clip_ids):
+    tile = (TILE, HEAD)
+    shape = jax.ShapeDtypeStruct(queries.shape, jnp.bfloat16)
+    bf16, f32 = jnp.bfloat16, jnp.float32
+    dma = pltpu.SemaphoreType.DMA
+    pairs = 10 * 3 * PER
+    return tuple(
+        pl.pallas_call(
+            functools.partial(head_kernel, n_high),
+            out_shape=(shape, shape, shape),
+            in_specs=[pl.BlockSpec(memory_space=pltpu.SMEM)] * 2
+            + [pl.BlockSpec(memory_space=pl.ANY)] * 4,
+            out_specs=(pl.BlockSpec(memory_space=pl.ANY),) * 3,
+            scratch_shapes=[
+                pltpu.VMEM((PER, 3, 2, ROWS) + tile, bf16),
+                pltpu.VMEM((PER, 2, ROWS) + tile, bf16),
+                pltpu.VMEM((WIN, TILE, 2 * TILE), f32),
+                pltpu.VMEM((WIN, TILE, 2 * TILE), f32),
+                pltpu.VMEM((HEAD, 2 * TILE), f32),
+                pltpu.VMEM((PER, 3, 2, ROWS) + tile, f32),
+                pltpu.VMEM((PER, 2, 2, ROWS) + tile, bf16),
+                pltpu.VMEM((PER, 2, 2, ROWS) + tile, bf16),
+                pltpu.VMEM((PER, 3, ROWS) + tile, bf16),
+                dma((PER, 4, ROWS)),
+                dma((PER, 4, ROWS)),
+                dma((PER, 2)),
+                dma((PER, 2)),
+                dma((PER, 2)),
+                dma((PER, 2)),
+                dma((PER, 3, ROWS)),
+                dma((PER, 3, ROWS)),
+            ],
+            compiler_params=pltpu.CompilerParams(
+                collective_id=0, has_side_effects=True, vmem_limit_bytes=48 * 1024 * 1024
+            ),
+            cost_estimate=pl.CostEstimate(
+                flops=pairs * 5 * 2 * TILE * TILE * HEAD,
+                bytes_accessed=7 * TILE * HD * 2,
+                transcendentals=pairs * TILE * TILE,
+            ),
+            name="head_parallel",
+        )(tile_counts, clip_ids, queries, keys, values, out_grad)
+    )
 
 
 def extended(block, sides, width):
@@ -128,8 +536,12 @@
         P(),
         P(),
     )
+    if mesh.shape["tm"] == ROWS:
+        body = functools.partial(by_heads, mesh.shape["height"])
+    else:
+        body = local
     return jax.shard_map(
-        local,
+        body,
         mesh=mesh,
         in_specs=placed,
         out_specs=(

time: 398 us -> 76.9 us (0.19)
  the two profiles are of different devices: /device:TPU:21 before, /device:TPU:1 now
where the time goes in v1:
time: 76.9 us; the launch traced here: 76.5 us
  Pallas kernels  67.8 us (88%)
  local copies, waits for them, and re-layouts  8.03 us (10%)
    pallas_call x1, Pallas kernels, by_heads(): pl.pallas_call(functools.partial(head_kernel, n_high), out_shape=(shape,...  67.8 us
    unnamed x15, local copies, waits for them, and re-layouts  8.03 us

profile of v1, /device:TPU:1, one launch (start us, length us, event | category | flops | bytes accessed | tf_op | source)
XLA Modules:
  0.0 76.5 jit_solution(5805196175593515755)
XLA Ops:
  0.6 0.0 copy-start
  0.6 1.1 %copy-done = bf16[1,1,192,1536]{3,2,1,0:T(8,128)(2,1)S(1)} copy-done((bf16[1,1,192,1536]{3,2,1,0:T(8,128)(2,1)S(1)}, bf16[1,1,192,1536]{3,2,1,0:T(8,128)(2,1)}, u32[]{:S(2)}) %copy-start) | copy-done | bytes 589848
  1.7 0.0 copy-start.1
  1.7 1.1 %copy-done.1 = bf16[1,1,192,1536]{3,2,1,0:T(8,128)(2,1)S(1)} copy-done((bf16[1,1,192,1536]{3,2,1,0:T(8,128)(2,1)S(1)}, bf16[1,1,192,1536]{3,2,1,0:T(8,128)(2,1)}, u32[]{:S(2)}) %copy-start.1) | copy-done | bytes 589848
  2.8 0.0 copy-start.2
  2.8 1.1 %copy-done.2 = bf16[1,1,192,1536]{3,2,1,0:T(8,128)(2,1)S(1)} copy-done((bf16[1,1,192,1536]{3,2,1,0:T(8,128)(2,1)S(1)}, bf16[1,1,192,1536]{3,2,1,0:T(8,128)(2,1)}, u32[]{:S(2)}) %copy-start.2) | copy-done | bytes 589848
  3.8 0.0 copy-start.3
  3.8 1.1 %copy-done.3 = bf16[1,1,192,1536]{3,2,1,0:T(8,128)(2,1)S(1)} copy-done((bf16[1,1,192,1536]{3,2,1,0:T(8,128)(2,1)S(1)}, bf16[1,1,192,1536]{3,2,1,0:T(8,128)(2,1)}, u32[]{:S(2)}) %copy-start.3) | copy-done | bytes 589848
  4.9 0.0 copy-start.4
  4.9 0.7 copy-done.4
  5.6 0.0 copy-start.5
  5.6 0.7 copy-done.5
  6.2 67.8 %head_parallel.1 = (bf16[1,1,192,1536]{3,2,1,0:T(8,128)(2,1)S(1)}, bf16[1,1,192,1536]{3,2,1,0:T(8,128)(2,1)S(1)}, bf16[1,1,192,1536]{3,2,1,0:T(8,128)(2,1)S(1)}) custom-call(s32[4,8]{1,0:T(4,128)S(1)} %copy-done.4, s32[4]{0:T(128)S(1)} %copy-done.5, bf16[1,1,192,1536]{3,2,1,0:T(8,128)(2,1)S(1)} %copy-done, bf16[1,1,192,1536]{3,2,1,0:T(8,128)(2,1)S(1)} %copy-done.1, ...), custom_call_target="tpu_custom_call" | custom-call | flops 4246732800 | bytes 4128768 | tf_op jit(solution)/shard_map/head_parallel/pallas_call | solution.py:382
  74.1 0.8 %copy.12 = bf16[1,1,192,1536]{3,2,1,0:T(8,128)(2,1)} copy(bf16[1,1,192,1536]{3,2,1,0:T(8,128)(2,1)S(1)} %get-tuple-element.6) | data formatting | bytes 1179648
  74.9 0.8 %copy.13 = bf16[1,1,192,1536]{3,2,1,0:T(8,128)(2,1)} copy(bf16[1,1,192,1536]{3,2,1,0:T(8,128)(2,1)S(1)} %get-tuple-element.7) | data formatting | bytes 1179648
  75.7 0.8 %copy.14 = bf16[1,1,192,1536]{3,2,1,0:T(8,128)(2,1)} copy(bf16[1,1,192,1536]{3,2,1,0:T(8,128)(2,1)S(1)} %get-tuple-element.8) | data formatting | bytes 1179648
Async XLA Ops:
  0.6 1.1 %copy-start = (bf16[1,1,192,1536]{3,2,1,0:T(8,128)(2,1)S(1)}, bf16[1,1,192,1536]{3,2,1,0:T(8,128)(2,1)}, u32[]{:S(2)}) copy-start(bf16[1,1,192,1536]{3,2,1,0:T(8,128)(2,1)} %q_in.1) | copy-start | bytes 1769476
  1.7 1.1 %copy-start.1 = (bf16[1,1,192,1536]{3,2,1,0:T(8,128)(2,1)S(1)}, bf16[1,1,192,1536]{3,2,1,0:T(8,128)(2,1)}, u32[]{:S(2)}) copy-start(bf16[1,1,192,1536]{3,2,1,0:T(8,128)(2,1)} %k_in.1) | copy-start | bytes 1769476
  2.8 1.1 %copy-start.2 = (bf16[1,1,192,1536]{3,2,1,0:T(8,128)(2,1)S(1)}, bf16[1,1,192,1536]{3,2,1,0:T(8,128)(2,1)}, u32[]{:S(2)}) copy-start(bf16[1,1,192,1536]{3,2,1,0:T(8,128)(2,1)} %v_in.1) | copy-start | bytes 1769476
  3.8 1.1 %copy-start.3 = (bf16[1,1,192,1536]{3,2,1,0:T(8,128)(2,1)S(1)}, bf16[1,1,192,1536]{3,2,1,0:T(8,128)(2,1)}, u32[]{:S(2)}) copy-start(bf16[1,1,192,1536]{3,2,1,0:T(8,128)(2,1)} %g_in.1) | copy-start | bytes 1769476
  4.9 0.7 copy-start.4
  5.6 0.7 copy-start.5

commit v2 on v1

--- a/solution.py
+++ b/solution.py
@@ -222,13 +222,13 @@
 
     def block(j, b):
         row = 2 * b
-        q = qg[j, 0, pl.ds(row, 2)].reshape(2 * TILE, HEAD)
-        g = qg[j, 1, pl.ds(row, 2)].reshape(2 * TILE, HEAD)
+        q = qg[j, 0, row : row + 2].reshape(2 * TILE, HEAD)
+        g = qg[j, 1, row : row + 2].reshape(2 * TILE, HEAD)
         q_t = q.T
         g_t = g.T
-
-        def scores(t, top):
-            key_row, offset = b + t // 3, t % 3
+        tiles = [(b + t // 3, t % 3) for t in range(WIN)]
+        top = jnp.full((8, 2 * TILE), -1e30, jnp.float32)
+        for t, (key_row, offset) in enumerate(tiles):
             s = jnp.dot(kv[j, offset, 0, key_row], q_t, preferred_element_type=jnp.float32)
             limit = jnp.where(
                 first_half,
@@ -237,45 +237,38 @@
             )
             s = jnp.where(slot < limit, s * (SCALE * math.log2(math.e)), jnp.float32(-1e30))
             score[t] = s
+            top = jnp.maximum(top, fold(s, jnp.max))
             pgrad[t] = jnp.dot(kv[j, offset, 1, key_row], g_t, preferred_element_type=jnp.float32)
-            return jnp.maximum(top, fold(s, jnp.max))
-
-        top = lax.fori_loop(0, WIN, scores, jnp.full((8, 2 * TILE), -1e30, jnp.float32))
         top = jnp.max(top, axis=0, keepdims=True)
-
-        def sums(t, carry):
-            total, dot = carry
+        total = jnp.zeros((8, 2 * TILE), jnp.float32)
+        dot = jnp.zeros((8, 2 * TILE), jnp.float32)
+        for t in range(WIN):
             e = jnp.exp2(score[t] - top)
             score[t] = e
-            return total + fold(e, jnp.sum), dot + fold(e * pgrad[t], jnp.sum)
-
-        zero = jnp.zeros((8, 2 * TILE), jnp.float32)
-        total, dot = lax.fori_loop(0, WIN, sums, (zero, zero))
+            total = total + fold(e, jnp.sum)
+            dot = dot + fold(e * pgrad[t], jnp.sum)
         total = jnp.sum(total, axis=0, keepdims=True)
         dot = jnp.sum(dot, axis=0, keepdims=True)
         own = jnp.where(first_half, counts[row, col], counts[row + 1, col] + TILE)
         inverse = 1.0 / total
         delta = dot * inverse
         inverse = jnp.where(lane < own, inverse, 0.0)
-        dq_t[...] = jnp.zeros_like(dq_t)
-
-        def grads(t, _):
-            key_row, offset = b + t // 3, t % 3
+        for t, (key_row, offset) in enumerate(tiles):
             p = score[t] * inverse
             ds = (p * (pgrad[t] - delta)).astype(jnp.bfloat16)
             p = p.astype(jnp.bfloat16)
             k_t = kv[j, offset, 0, key_row].T
-            dq_t[...] += jnp.dot(k_t, ds, preferred_element_type=jnp.float32)
-            fresh = (b == 0) | (key_row == ROWS - 1)
-            old_k = jnp.where(fresh, 0.0, acc[j, offset, 0, key_row])
-            acc[j, offset, 0, key_row] = old_k + jnp.dot(ds, q, preferred_element_type=jnp.float32)
-            old_v = jnp.where(fresh, 0.0, acc[j, offset, 1, key_row])
-            acc[j, offset, 1, key_row] = old_v + jnp.dot(p, g, preferred_element_type=jnp.float32)
-            return 0
-
-        lax.fori_loop(0, WIN, grads, 0)
+            dq = jnp.dot(k_t, ds, preferred_element_type=jnp.float32)
+            dq_t[...] = dq if t == 0 else dq_t[...] + dq
+            dk = jnp.dot(ds, q, preferred_element_type=jnp.float32)
+            dv = jnp.dot(p, g, preferred_element_type=jnp.float32)
+            if b > 0 and key_row < ROWS - 1:
+                dk = dk + acc[j, offset, 0, key_row]
+                dv = dv + acc[j, offset, 1, key_row]
+            acc[j, offset, 0, key_row] = dk
+            acc[j, offset, 1, key_row] = dv
         dq = (dq_t[...] * SCALE).T.astype(jnp.bfloat16)
-        o_send[j, 0, pl.ds(row, 2)] = dq.reshape(2, TILE, HEAD)
+        o_send[j, 0, row : row + 2] = dq.reshape(2, TILE, HEAD)
 
     def send_terms(j):
         for side, there, step in sides:
@@ -334,11 +327,9 @@
             def _():
                 kv_arrival(j, side, step).wait_recv()
 
-        def one_block(b, _):
+        for b in range(ROWS // 2):
             block(j, b)
-            return 0
-
-        lax.fori_loop(0, ROWS // 2, one_block, 0)
+
         send_terms(j)
         start_out(j, 0)
 
@@ -383,8 +374,8 @@
             functools.partial(head_kernel, n_high),
             out_shape=(shape, shape, shape),
             in_specs=[pl.BlockSpec(memory_space=pltpu.SMEM)] * 2
-            + [pl.BlockSpec(memory_space=pl.ANY)] * 4,
-            out_specs=(pl.BlockSpec(memory_space=pl.ANY),) * 3,
+            + [pl.BlockSpec(memory_space=pltpu.HBM)] * 4,
+            out_specs=(pl.BlockSpec(memory_space=pltpu.HBM),) * 3,
             scratch_shapes=[
                 pltpu.VMEM((PER, 3, 2, ROWS) + tile, bf16),
                 pltpu.VMEM((PER, 2, ROWS) + tile, bf16),
@@ -405,7 +396,7 @@
                 dma((PER, 3, ROWS)),
             ],
             compiler_params=pltpu.CompilerParams(
-                collective_id=0, has_side_effects=True, vmem_limit_bytes=48 * 1024 * 1024
+                collective_id=0, has_side_effects=True, vmem_limit_bytes=63 * 1024 * 1024
             ),
             cost_estimate=pl.CostEstimate(
                 flops=pairs * 5 * 2 * TILE * TILE * HEAD,

time: 76.9 us -> 60.3 us (0.78)
  Pallas kernels: 67.8 us -> 55.3 us
  local copies, waits for them, and re-layouts: 8.03 us -> 4.07 us
    pallas_call x1, Pallas kernels: 67.8 us -> 55.3 us  [by_heads(): pl.pallas_call(functools.partial(head_kernel, n_high), out_shape=(shape,...]
    unnamed x15 -> x7, local copies, waits for them, and re-layouts: 8.03 us -> 4.07 us
where the time goes in v2:
time: 60.3 us; the launch traced here: 60 us
  Pallas kernels  55.3 us (92%)
  local copies, waits for them, and re-layouts  4.07 us (7%)
  between operations  0.65 us (1%)
    pallas_call x1, Pallas kernels, by_heads(): pl.pallas_call(functools.partial(head_kernel, n_high), out_shape=(shape,...  55.3 us
    unnamed x7, local copies, waits for them, and re-layouts  4.07 us

profile of v2, /device:TPU:1, one launch (start us, length us, event | category | flops | bytes accessed | tf_op | source)
XLA Modules:
  0.0 60.0 jit_solution(6707599830192215596)
XLA Ops:
  0.6 55.3 %head_parallel.1 = (bf16[1,1,192,1536]{3,2,1,0:T(8,128)(2,1)}, bf16[1,1,192,1536]{3,2,1,0:T(8,128)(2,1)}, bf16[1,1,192,1536]{3,2,1,0:T(8,128)(2,1)}) custom-call(s32[4,8]{1,0:T(4,128)} %counts.1, s32[4]{0:T(128)} %clips.1, bf16[1,1,192,1536]{3,2,1,0:T(8,128)(2,1)} %q_in.1, bf16[1,1,192,1536]{3,2,1,0:T(8,128)(2,1)} %k_in.1, bf16[1,1,192,1536]{3,2,1,0:T(8,128)(2,1)} %v_in.1, ...), custom_call_target="tpu_custom_call" | custom-call | flops 4246732800 | bytes 4128768 | tf_op jit(solution)/shard_map/head_parallel/pallas_call | solution.py:373
  55.9 0.0 copy-start.1
  55.9 2.0 %copy.12 = bf16[1,1,192,1536]{3,2,1,0:T(8,128)(2,1)} copy(bf16[1,1,192,1536]{3,2,1,0:T(8,128)(2,1)} %get-tuple-element.6) | data formatting | bytes 1179648
  57.9 0.0 copy-done.1
  57.9 0.0 copy-start
  57.9 0.8 %copy.13 = bf16[1,1,192,1536]{3,2,1,0:T(8,128)(2,1)} copy(bf16[1,1,192,1536]{3,2,1,0:T(8,128)(2,1)S(1)} %copy-done.1) | data formatting | bytes 1179648
  58.7 0.5 copy-done
  59.2 0.8 %copy.14 = bf16[1,1,192,1536]{3,2,1,0:T(8,128)(2,1)} copy(bf16[1,1,192,1536]{3,2,1,0:T(8,128)(2,1)S(1)} %copy-done) | data formatting | bytes 1179648
Async XLA Ops:
  55.9 2.0 %copy-start.1 = (bf16[1,1,192,1536]{3,2,1,0:T(8,128)(2,1)S(1)}, bf16[1,1,192,1536]{3,2,1,0:T(8,128)(2,1)}, u32[]{:S(2)}) copy-start(bf16[1,1,192,1536]{3,2,1,0:T(8,128)(2,1)} %get-tuple-element.7) | copy-start | bytes 1769476
  57.9 1.3 %copy-start = (bf16[1,1,192,1536]{3,2,1,0:T(8,128)(2,1)S(1)}, bf16[1,1,192,1536]{3,2,1,0:T(8,128)(2,1)}, u32[]{:S(2)}) copy-start(bf16[1,1,192,1536]{3,2,1,0:T(8,128)(2,1)} %get-tuple-element.8) | copy-start | bytes 1769476

commit v3 on v2

--- a/solution.py
+++ b/solution.py
@@ -16,13 +16,14 @@
 SCALE = 1.0 / HEAD**0.5
 ROWS = 4
 PER = HEADS // ROWS
+PIECES = 2
 WIN = 9
 
 
 def head_kernel(
     n_high,
-    counts,
-    clips,
+    counts_in,
+    clips_in,
     q_in,
     k_in,
     v_in,
@@ -39,6 +40,9 @@
     t_send,
     t_recv,
     o_send,
+    counts,
+    clips,
+    small,
     in_send,
     in_recv,
     kv_send,
@@ -54,6 +58,13 @@
     has_high = col < n_high - 1
     peers = [lax.rem(me + i, ROWS) for i in (1, 2, 3)]
 
+    small_copies = (
+        pltpu.make_async_copy(counts_in, counts, small.at[0]),
+        pltpu.make_async_copy(clips_in, clips, small.at[1]),
+    )
+    for copy in small_copies:
+        copy.start()
+
     barrier = pltpu.get_barrier_semaphore()
     for peer in peers:
         pl.semaphore_signal(barrier, inc=1, device_id=(peer, col), device_id_type=MESH)
@@ -220,13 +231,23 @@
     def fold(x, op):
         return op(x.reshape(TILE // 8, 8, 2 * TILE), axis=0)
 
+    def send_terms(j, which):
+        side, there, step = sides[which]
+
+        @pl.when(there)
+        def _():
+            for r in range(ROWS):
+                t_send[j, side, 0, r] = (acc[j, 2 * side, 0, r] * SCALE).astype(jnp.bfloat16)
+                t_send[j, side, 1, r] = acc[j, 2 * side, 1, r].astype(jnp.bfloat16)
+            term_copy(j, side, step).start()
+
     def block(j, b):
         row = 2 * b
         q = qg[j, 0, row : row + 2].reshape(2 * TILE, HEAD)
         g = qg[j, 1, row : row + 2].reshape(2 * TILE, HEAD)
         q_t = q.T
         g_t = g.T
-        tiles = [(b + t // 3, t % 3) for t in range(WIN)]
+        tiles = [(b + t % 3, (0, 2, 1)[t // 3]) for t in range(WIN)]
         top = jnp.full((8, 2 * TILE), -1e30, jnp.float32)
         for t, (key_row, offset) in enumerate(tiles):
             s = jnp.dot(kv[j, offset, 0, key_row], q_t, preferred_element_type=jnp.float32)
@@ -267,21 +288,10 @@
                 dv = dv + acc[j, offset, 1, key_row]
             acc[j, offset, 0, key_row] = dk
             acc[j, offset, 1, key_row] = dv
+            if b == ROWS // 2 - 1 and t in (2, 5):
+                send_terms(j, t // 5)
         dq = (dq_t[...] * SCALE).T.astype(jnp.bfloat16)
         o_send[j, 0, row : row + 2] = dq.reshape(2, TILE, HEAD)
-
-    def send_terms(j):
-        for side, there, step in sides:
-
-            @pl.when(there)
-            def _():
-                def cast(r, _):
-                    t_send[j, side, 0, r] = (acc[j, 2 * side, 0, r] * SCALE).astype(jnp.bfloat16)
-                    t_send[j, side, 1, r] = acc[j, 2 * side, 1, r].astype(jnp.bfloat16)
-                    return 0
-
-                lax.fori_loop(0, ROWS, cast, 0)
-                term_copy(j, side, step).start()
 
     def finish(j):
         for side, there, step in sides:
@@ -313,6 +323,9 @@
         start_out(j, 1)
         start_out(j, 2)
 
+    for copy in small_copies:
+        copy.wait()
+
     forward(0)
 
     def head(j, _):
@@ -330,7 +343,6 @@
         for b in range(ROWS // 2):
             block(j, b)
 
-        send_terms(j)
         start_out(j, 0)
 
         @pl.when(j > 0)
@@ -363,18 +375,40 @@
     lax.fori_loop(0, PER, drain, 0)
 
 
+def place_kernel(dq, dk, dv, dq_out, dk_out, dv_out, held, sem):
+    rows = TILE // PIECES
+    copies = [
+        (
+            pltpu.make_async_copy(
+                source.at[0, 0, pl.ds(i * rows, rows)], held.at[a, i], sem.at[0, a, i]
+            ),
+            pltpu.make_async_copy(
+                held.at[a, i], target.at[0, 0, pl.ds(i * rows, rows)], sem.at[1, a, i]
+            ),
+        )
+        for a, (source, target) in enumerate(((dq, dq_out), (dk, dk_out), (dv, dv_out)))
+        for i in range(PIECES)
+    ]
+    for arrive, _ in copies:
+        arrive.start()
+    for arrive, leave in copies:
+        arrive.wait()
+        leave.start()
+    for _, leave in copies:
+        leave.wait()
+
+
 def by_heads(n_high, queries, keys, values, out_grad, tile_counts, clip_ids):
     tile = (TILE, HEAD)
     shape = jax.ShapeDtypeStruct(queries.shape, jnp.bfloat16)
     bf16, f32 = jnp.bfloat16, jnp.float32
     dma = pltpu.SemaphoreType.DMA
     pairs = 10 * 3 * PER
-    return tuple(
+    parts = (
         pl.pallas_call(
             functools.partial(head_kernel, n_high),
             out_shape=(shape, shape, shape),
-            in_specs=[pl.BlockSpec(memory_space=pltpu.SMEM)] * 2
-            + [pl.BlockSpec(memory_space=pltpu.HBM)] * 4,
+            in_specs=[pl.BlockSpec(memory_space=pltpu.HBM)] * 6,
             out_specs=(pl.BlockSpec(memory_space=pltpu.HBM),) * 3,
             scratch_shapes=[
                 pltpu.VMEM((PER, 3, 2, ROWS) + tile, bf16),
@@ -386,6 +420,9 @@
                 pltpu.VMEM((PER, 2, 2, ROWS) + tile, bf16),
                 pltpu.VMEM((PER, 2, 2, ROWS) + tile, bf16),
                 pltpu.VMEM((PER, 3, ROWS) + tile, bf16),
+                pltpu.SMEM(tile_counts.shape, jnp.int32),
+                pltpu.SMEM(clip_ids.shape, jnp.int32),
+                dma((2,)),
                 dma((PER, 4, ROWS)),
                 dma((PER, 4, ROWS)),
                 dma((PER, 2)),
@@ -405,6 +442,22 @@
             ),
             name="head_parallel",
         )(tile_counts, clip_ids, queries, keys, values, out_grad)
+    )
+    return tuple(
+        pl.pallas_call(
+            place_kernel,
+            out_shape=(shape, shape, shape),
+            in_specs=[pl.BlockSpec(memory_space=pl.ANY)] * 3,
+            out_specs=(pl.BlockSpec(memory_space=pl.ANY),) * 3,
+            scratch_shapes=[
+                pltpu.VMEM((3, PIECES, TILE // PIECES, HD), bf16),
+                dma((2, 3, PIECES)),
+            ],
+            cost_estimate=pl.CostEstimate(
+                flops=0, bytes_accessed=6 * TILE * HD * 2, transcendentals=0
+            ),
+            name="place",
+        )(*parts)
     )
 
 

time: 60.3 us -> 57.5 us (0.954)
  local copies, waits for them, and re-layouts: 4.07 us -> 0 us
  Pallas kernels: 55.3 us -> 56.6 us
    unnamed x7 -> x0, local copies, waits for them, and re-layouts: 4.07 us -> none
    pallas_call x0 -> x1, Pallas kernels: none -> 2.27 us  [by_heads(): pl.pallas_call(place_kernel, out_shape=(shape, shape, shape), in_specs=[p...]
    pallas_call x1, Pallas kernels: 55.3 us -> 54.4 us  [by_heads(): pl.pallas_call(functools.partial(head_kernel, n_high), out_shape=(shape,...]
where the time goes in v3:
time: 57.5 us; the launch traced here: 57.3 us
  Pallas kernels  56.6 us (98%)
  between operations  0.64 us (1%)
    pallas_call x1, Pallas kernels, by_heads(): pl.pallas_call(functools.partial(head_kernel, n_high), out_shape=(shape,...  54.4 us
    pallas_call x1, Pallas kernels, by_heads(): pl.pallas_call(place_kernel, out_shape=(shape, shape, shape), in_specs=[p...  2.27 us

profile of v3, /device:TPU:1, one launch (start us, length us, event | category | flops | bytes accessed | tf_op | source)
XLA Modules:
  0.0 57.3 jit_solution(10007237992533192408)
XLA Ops:
  0.6 54.4 %head_parallel.1 = (bf16[1,1,192,1536]{3,2,1,0:T(8,128)(2,1)}, bf16[1,1,192,1536]{3,2,1,0:T(8,128)(2,1)}, bf16[1,1,192,1536]{3,2,1,0:T(8,128)(2,1)}) custom-call(s32[4,8]{1,0:T(4,128)} %counts_in.1, s32[4]{0:T(128)} %clips_in.1, bf16[1,1,192,1536]{3,2,1,0:T(8,128)(2,1)} %q_in.1, bf16[1,1,192,1536]{3,2,1,0:T(8,128)(2,1)} %k_in.1, ...), custom_call_target="tpu_custom_call" | custom-call | flops 4246732800 | bytes 4128768 | tf_op jit(solution)/shard_map/head_parallel/pallas_call | solution.py:408
  55.0 2.3 %place.1 = (bf16[1,1,192,1536]{3,2,1,0:T(8,128)(2,1)}, bf16[1,1,192,1536]{3,2,1,0:T(8,128)(2,1)}, bf16[1,1,192,1536]{3,2,1,0:T(8,128)(2,1)}) custom-call(bf16[1,1,192,1536]{3,2,1,0:T(8,128)(2,1)} %get-tuple-element.6.dq, bf16[1,1,192,1536]{3,2,1,0:T(8,128)(2,1)} %get-tuple-element.7.dk, bf16[1,1,192,1536]{3,2,1,0:T(8,128)(2,1)} %get-tuple-element.8.dv), custom_call_target="tpu_custom_call" | custom-call | bytes 3538944 | tf_op jit(solution)/shard_map/place/pallas_call | solution.py:447
